TPU v7x, 512 devices: a whole 4x8x8 slice. The times are simulated.
512 devices in a mesh: leaf: 512 (over x, y, z, core).
Axes of the slice: x: 4, y: 8, z: 8, core: 2. Of those that a mesh axis runs over, the one named last changes fastest.
Arguments:
- features: bfloat16 [262144, 1024], P('leaf'), may hold values from -6 to 6
- probes: float32 [262144, 128], P('leaf'), may hold values from -6 to 6
- bases: float32 [262144, 256], P('leaf'), may hold values from -0.25 to 0.25
- transfers: float32 [512, 4, 256, 256], P('leaf'), may hold values from -1 to 1, as said below
- couplings: float32 [512, 5, 256, 256], P('leaf'), may hold values from -1 to 1, as said below
- near_list: int32 [512, 4], P('leaf'), may hold values from 0 to 511, as said below
- near_count: int32 [512], P('leaf'), may hold values from 1 to 4
Outputs:
- product: float32 [262144, 128], P('leaf')
Inputs may be any that keep to these rules, and one draw needn't show every extreme that they name: `near_list`: the first near_count[i] entries of row i are distinct leaves other than i, each at most 2 from i; the other entries equal i. Some leaf lists 4 leaves. transfers[i, l] is the same for all leaves i of one node of level l (an aligned block of 2^l leaves). couplings[i, l] is the same for all leaves i of one node of level l (an aligned block of 2^l leaves).
All inputs are finite; a program needn't handle non-finite values.
Results may differ from a plain program's by a relative error of at most 0.00095.
Values may be sent and summed in bfloat16 or wider, within the bound.
A program may use at most 64 MiB of HBM per device.

v0:
```python
import jax
import jax.numpy as jnp
from jax import lax
from jax.sharding import PartitionSpec as P


def from_behind(array, axis, by):
    peers = lax.axis_size(axis)
    pairs = [(i, i + by) for i in range(peers) if 0 <= i + by < peers]
    return lax.ppermute(array, axis, pairs)


def partner(array, axis, distance):
    return lax.ppermute(array, axis, [(i, i ^ 1 << distance) for i in range(lax.axis_size(axis))])


def kernel_tile(rows_a, rows_b):
    gram_tile = lax.dot_general(
        rows_a, rows_b, (((1,), (1,)), ((), ())), preferred_element_type=jnp.float32
    )
    return gram_tile * gram_tile * (1.0 / (rows_a.shape[1] * rows_a.shape[0]))


def contract_first(matrix, values):
    return lax.dot_general(
        matrix,
        values,
        (((0,), (0,)), ((), ())),
        precision=lax.Precision.HIGHEST,
        preferred_element_type=jnp.float32,
    )


def apply_matrix(matrix, values):
    return jnp.dot(
        matrix, values, precision=lax.Precision.HIGHEST, preferred_element_type=jnp.float32
    )


def shards(features, probes, bases, transfers, couplings, near_list, near_count):
    leaf_index = lax.axis_index("leaf")
    tree_depth = transfers.shape[1]
    scale_g = (3.0 / transfers.shape[-1]) ** 0.5
    near_span = near_list.shape[1] // 2
    slot_ids = jnp.arange(near_list.shape[1], dtype=jnp.int32)
    is_live = slot_ids < near_count[0]

    def member(offset):
        return jnp.any((near_list[0] == leaf_index + offset) & is_live).astype(jnp.float32)

    near_sum = apply_matrix(kernel_tile(features, features), probes)
    for offset in range(1, near_span + 1):
        remote = from_behind(features, "leaf", -offset)
        remote_x = from_behind(probes.astype(jnp.bfloat16), "leaf", -offset).astype(probes.dtype)
        kernel = kernel_tile(features, remote)
        near_sum = near_sum + member(offset) * apply_matrix(kernel, remote_x)
        back_term = contract_first(kernel, probes)
        returned = from_behind(back_term, "leaf", offset)
        near_sum = near_sum + member(-offset) * returned
    skeleton = contract_first(bases, probes)
    levels = [skeleton]
    siblings = []
    for height in range(1, tree_depth + 1):
        factor = scale_g * 2.0 ** (-0.5 * height)
        pieces = factor * contract_first(transfers[0, height - 1], levels[-1])
        levels.append(
            pieces + partner(pieces.astype(jnp.bfloat16), "leaf", height - 1).astype(pieces.dtype)
        )
    for height in range(tree_depth + 1):
        siblings.append(partner(levels[height], "leaf", height))
    expansion = None
    for height in range(tree_depth, -1, -1):
        update = scale_g * apply_matrix(couplings[0, height], siblings[height])
        if height < tree_depth:
            update = update + scale_g * 2.0 ** (-0.5 * (height + 1)) * apply_matrix(
                transfers[0, height], expansion
            )
        expansion = update
    far_sum = apply_matrix(bases, expansion)
    return near_sum + far_sum


def solution(mesh):
    in_specs = (
        P("leaf", None),
        P("leaf", None),
        P("leaf", None),
        P("leaf", None, None, None),
        P("leaf", None, None, None),
        P("leaf", None),
        P("leaf"),
    )
    out_specs = P("leaf", None)
    return jax.shard_map(shards, mesh=mesh, in_specs=in_specs, out_specs=out_specs, check_vma=False)
```

profile of v0, /device:TPU:6, one launch (start us, length us, event | category | flops | bytes accessed | tf_op | source)
XLA Modules:
  0.0 140.9 jit_solution(699100893715465417)
XLA Ops:
  0.0 0.0 copy-start
  0.0 1.0 copy-done
  1.0 1.9 %fusion.53 = f32[256,128]{1,0:T(8,128)S(1)} fusion(f32[512,256]{1,0:T(8,128)S(1)} %copy-done, f32[512,128]{1,0:T(8,128)} %param.8), kind=kOutput, calls=%fused_computation.81 | convolution fusion | flops 201326592 | bytes 917504 | tf_op jit(solution)/shard_map/dot_general | solution.py:25
  3.0 0.0 copy-start.1
  3.0 1.4 fusion.46
  4.4 1.9 %collective-permute-start.7 = (bf16[256,128]{0,1:T(8,128)(2,1)S(1)}, bf16[256,128]{0,1:T(8,128)(2,1)S(1)}, u32[]{:S(2)}, u32[]{:S(2)}) collective-permute-start(bf16[256,128]{0,1:T(8,128)(2,1)S(1)} %get-tuple-element.9), channel_id=1, source_target_pairs={{0,1},{1,0},{2,3},{3,2},{4,5},{5,4},{6,7},{7,6},{8,9},{9,8},{10,11... | collective-permute-start | bytes 196616 | tf_op jit(solution)/shard_map/ppermute | solution.py:14
  6.3 1.2 collective-permute-done.7
  7.6 0.3 fusion.47
  7.9 4.3 %collective-permute-start.9 = (bf16[256,128]{0,1:T(8,128)(2,1)S(1)}, bf16[256,128]{0,1:T(8,128)(2,1)S(1)}, u32[]{:S(2)}, u32[]{:S(2)}) collective-permute-start(bf16[256,128]{0,1:T(8,128)(2,1)S(1)} %get-tuple-element.11), channel_id=1, source_target_pairs={{0,2},{1,3},{2,0},{3,1},{4,6},{5,7},{6,4},{7,5},{8,10},{9,11},{10,... | collective-permute-start | bytes 196616 | tf_op jit(solution)/shard_map/ppermute | solution.py:14
  12.2 2.4 %collective-permute-done.9 = bf16[256,128]{0,1:T(8,128)(2,1)S(1)} collective-permute-done((bf16[256,128]{0,1:T(8,128)(2,1)S(1)}, bf16[256,128]{0,1:T(8,128)(2,1)S(1)}, u32[]{:S(2)}, u32[]{:S(2)}) %collective-permute-start.9) | collective-permute-done | bytes 65568 | tf_op jit(solution)/shard_map/ppermute | solution.py:14
  14.6 0.3 fusion.48
  14.9 6.1 %collective-permute-start.11 = (bf16[256,128]{0,1:T(8,128)(2,1)S(1)}, bf16[256,128]{0,1:T(8,128)(2,1)S(1)}, u32[]{:S(2)}, u32[]{:S(2)}) collective-permute-start(bf16[256,128]{0,1:T(8,128)(2,1)S(1)} %get-tuple-element.13), channel_id=1, source_target_pairs={{0,4},{1,5},{2,6},{3,7},{4,0},{5,1},{6,2},{7,3},{8,12},{9,13},{10,... | collective-permute-start | bytes 196616 | tf_op jit(solution)/shard_map/ppermute | solution.py:14
  21.0 1.9 %collective-permute-start.6 = (f32[256,128]{1,0:T(8,128)S(1)}, f32[256,128]{1,0:T(8,128)}, u32[]{:S(2)}, u32[]{:S(2)}) collective-permute-start(f32[256,128]{1,0:T(8,128)S(1)} %fusion.53), channel_id=1, source_target_pairs={{0,1},{1,0},{2,3},{3,2},{4,5},{5,4},{6,7},{7,6},{8,9},{9,8},{10,11... | collective-permute-start | bytes 393224 | tf_op jit(solution)/shard_map/ppermute | solution.py:14
  22.9 10.0 %collective-permute-start.3 = (bf16[512,1024]{1,0:T(8,128)(2,1)}, bf16[512,1024]{1,0:T(8,128)(2,1)}, u32[]{:S(2)}, u32[]{:S(2)}) collective-permute-start(bf16[512,1024]{1,0:T(8,128)(2,1)} %param.7), channel_id=1, source_target_pairs={{2,0},{3,1},{4,2},{5,3},{6,4},{7,5},{8,6},{9,7},{10,8},{11,9},{12,... | collective-permute-start | bytes 3145736 | tf_op jit(solution)/shard_map/ppermute | solution.py:10
  32.9 2.3 %collective-permute-start = (bf16[512,1024]{1,0:T(8,128)(2,1)}, bf16[512,1024]{1,0:T(8,128)(2,1)}, u32[]{:S(2)}, u32[]{:S(2)}) collective-permute-start(bf16[512,1024]{1,0:T(8,128)(2,1)} %param.7), channel_id=1, source_target_pairs={{1,0},{2,1},{3,2},{4,3},{5,4},{6,5},{7,6},{8,7},{9,8},{10,9},{11,1... | collective-permute-start | bytes 3145736 | tf_op jit(solution)/shard_map/ppermute | solution.py:10
  35.2 0.7 convert_element_type.43
  35.8 4.3 %collective-permute-start.4 = (bf16[512,128]{1,0:T(8,128)(2,1)}, bf16[512,128]{1,0:T(8,128)(2,1)}, u32[]{:S(2)}, u32[]{:S(2)}) collective-permute-start(bf16[512,128]{1,0:T(8,128)(2,1)} %convert_element_type.43), channel_id=1, source_target_pairs={{2,0},{3,1},{4,2},{5,3},{6,4},{7,5},{8,6},{9,7},{10,8},{11,9},{12,... | collective-permute-start | bytes 393224 | tf_op jit(solution)/shard_map/ppermute | solution.py:10
  40.1 0.0 collective-permute-done.11
  40.2 0.3 fusion.49
  40.5 0.3 copy-done.7
  40.8 1.9 %collective-permute-start.13 = (bf16[256,128]{0,1:T(8,128)(2,1)S(1)}, bf16[256,128]{0,1:T(8,128)(2,1)S(1)}, u32[]{:S(2)}, u32[]{:S(2)}) collective-permute-start(bf16[256,128]{0,1:T(8,128)(2,1)S(1)} %get-tuple-element.15), channel_id=1, source_target_pairs={{0,8},{1,9},{2,10},{3,11},{4,12},{5,13},{6,14},{7,15},{8,0},{9,1},... | collective-permute-start | bytes 196616 | tf_op jit(solution)/shard_map/ppermute | solution.py:14
  42.7 2.6 %fusion = f32[512,512]{1,0:T(8,128)S(1)} fusion(bf16[512,1024]{1,0:T(8,128)(2,1)} %param.7), kind=kOutput, calls=%fused_computation.3 | convolution fusion | flops 537395200 | bytes 2097152 | tf_op jit(solution)/shard_map/dot_general | solution.py:18
  45.3 0.0 copy-start.8
  45.3 0.0 copy-start.3
  45.4 5.5 %collective-permute-done.13 = bf16[256,128]{0,1:T(8,128)(2,1)S(1)} collective-permute-done((bf16[256,128]{0,1:T(8,128)(2,1)S(1)}, bf16[256,128]{0,1:T(8,128)(2,1)S(1)}, u32[]{:S(2)}, u32[]{:S(2)}) %collective-permute-start.13) | collective-permute-done | bytes 65568 | tf_op jit(solution)/shard_map/ppermute | solution.py:14
  50.9 0.7 convert_add_fusion
  51.6 1.9 %collective-permute-start.14 = (f32[256,128]{0,1:T(8,128)}, f32[256,128]{0,1:T(8,128)}, u32[]{:S(2)}, u32[]{:S(2)}) collective-permute-start(f32[256,128]{0,1:T(8,128)} %convert_add_fusion), channel_id=1, source_target_pairs={{0,16},{1,17},{2,18},{3,19},{4,20},{5,21},{6,22},{7,23},{8,24},{9,... | collective-permute-start | bytes 393224 | tf_op jit(solution)/shard_map/ppermute | solution.py:14
  53.5 1.0 fusion.50
  55.1 0.0 copy-done.8
  55.1 0.7 fusion.45
  58.3 16.2 %collective-permute-done.14 = f32[256,128]{0,1:T(8,128)} collective-permute-done((f32[256,128]{0,1:T(8,128)}, f32[256,128]{0,1:T(8,128)}, u32[]{:S(2)}, u32[]{:S(2)}) %collective-permute-start.14) | collective-permute-done | bytes 131104 | tf_op jit(solution)/shard_map/ppermute | solution.py:14
  74.5 1.9 %collective-permute-start.12 = (f32[256,128]{0,1:T(8,128)}, f32[256,128]{0,1:T(8,128)S(1)}, u32[]{:S(2)}, u32[]{:S(2)}) collective-permute-start(f32[256,128]{0,1:T(8,128)} %copy-done.7), channel_id=1, source_target_pairs={{0,8},{1,9},{2,10},{3,11},{4,12},{5,13},{6,14},{7,15},{8,0},{9,1},... | collective-permute-start | bytes 393224 | tf_op jit(solution)/shard_map/ppermute | solution.py:14
  76.5 0.0 copy-done.3
  76.5 1.3 convolution_multiply_fusion.9
  77.8 0.4 convolution_multiply_fusion.8
  78.2 7.4 %collective-permute-done.12 = f32[256,128]{0,1:T(8,128)S(1)} collective-permute-done((f32[256,128]{0,1:T(8,128)}, f32[256,128]{0,1:T(8,128)S(1)}, u32[]{:S(2)}, u32[]{:S(2)}) %collective-permute-start.12) | collective-permute-done | bytes 131104 | tf_op jit(solution)/shard_map/ppermute | solution.py:14
  85.6 1.9 %collective-permute-start.10 = (f32[256,128]{0,1:T(8,128)}, f32[256,128]{0,1:T(8,128)S(1)}, u32[]{:S(2)}, u32[]{:S(2)}) collective-permute-start(f32[256,128]{0,1:T(8,128)} %copy-done.6), channel_id=1, source_target_pairs={{0,4},{1,5},{2,6},{3,7},{4,0},{5,1},{6,2},{7,3},{8,12},{9,13},{10,... | collective-permute-start | bytes 393224 | tf_op jit(solution)/shard_map/ppermute | solution.py:14
  87.5 0.4 fusion.9
  87.9 0.4 convolution_multiply_fusion.7
  88.3 5.7 %collective-permute-done.10 = f32[256,128]{0,1:T(8,128)S(1)} collective-permute-done((f32[256,128]{0,1:T(8,128)}, f32[256,128]{0,1:T(8,128)S(1)}, u32[]{:S(2)}, u32[]{:S(2)}) %collective-permute-start.10) | collective-permute-done | bytes 131104 | tf_op jit(solution)/shard_map/ppermute | solution.py:14
  94.0 13.1 %collective-permute-start.8 = (f32[256,128]{0,1:T(8,128)S(1)}, f32[256,128]{0,1:T(8,128)S(1)}, u32[]{:S(2)}, u32[]{:S(2)}) collective-permute-start(f32[256,128]{0,1:T(8,128)S(1)} %copy-done.5), channel_id=1, source_target_pairs={{0,2},{1,3},{2,0},{3,1},{4,6},{5,7},{6,4},{7,5},{8,10},{9,11},{10,... | collective-permute-start | bytes 393224 | tf_op jit(solution)/shard_map/ppermute | solution.py:14
  107.1 0.4 fusion.11
  107.5 0.4 convolution_multiply_fusion.6
  107.9 2.1 %collective-permute-done.8 = f32[256,128]{0,1:T(8,128)S(1)} collective-permute-done((f32[256,128]{0,1:T(8,128)S(1)}, f32[256,128]{0,1:T(8,128)S(1)}, u32[]{:S(2)}, u32[]{:S(2)}) %collective-permute-start.8) | collective-permute-done | bytes 131104 | tf_op jit(solution)/shard_map/ppermute | solution.py:14
  110.0 1.9 %collective-permute-start.1 = (bf16[512,128]{1,0:T(8,128)(2,1)}, bf16[512,128]{1,0:T(8,128)(2,1)S(1)}, u32[]{:S(2)}, u32[]{:S(2)}) collective-permute-start(bf16[512,128]{1,0:T(8,128)(2,1)} %convert_element_type.43), channel_id=1, source_target_pairs={{1,0},{2,1},{3,2},{4,3},{5,4},{6,5},{7,6},{8,7},{9,8},{10,9},{11,1... | collective-permute-start | bytes 393224 | tf_op jit(solution)/shard_map/ppermute | solution.py:10
  111.9 0.4 fusion.13
  112.3 0.4 convolution_multiply_fusion.5
  112.7 0.0 collective-permute-done.6
  112.8 1.3 fusion.15
  114.1 0.0 collective-permute-done
  114.1 2.3 %fusion.1 = f32[512,512]{1,0:T(8,128)S(1)} fusion(bf16[512,1024]{1,0:T(8,128)(2,1)} %param.7, bf16[512,1024]{1,0:T(8,128)(2,1)} %collective-permute-done), kind=kOutput, calls=%fused_computation.4 | convolution fusion | flops 537395200 | bytes 3145728 | tf_op jit(solution)/shard_map/dot_general | solution.py:18
  116.4 1.8 %fusion.51 = f32[512,128]{1,0:T(8,128)S(1)} fusion(f32[512,512]{1,0:T(8,128)S(1)} %fusion.1, f32[512,128]{1,0:T(8,128)S(1)} %copy-done.1), kind=kOutput, calls=%fused_computation.79 | convolution fusion | flops 402653184 | bytes 1572864 | tf_op jit(solution)/shard_map/dot_general | solution.py:25
  118.2 2.6 %collective-permute-start.2 = (f32[512,128]{1,0:T(8,128)S(1)}, f32[512,128]{1,0:T(8,128)S(1)}, u32[]{:S(2)}, u32[]{:S(2)}) collective-permute-start(f32[512,128]{1,0:T(8,128)S(1)} %fusion.51), channel_id=1, source_target_pairs={{0,1},{1,2},{2,3},{3,4},{4,5},{5,6},{6,7},{7,8},{8,9},{9,10},{10,1... | collective-permute-start | bytes 786440 | tf_op jit(solution)/shard_map/ppermute | solution.py:10
  120.8 0.0 collective-permute-done.3
  120.8 2.3 %fusion.2 = f32[512,512]{1,0:T(8,128)S(1)} fusion(bf16[512,1024]{1,0:T(8,128)(2,1)} %param.7, bf16[512,1024]{1,0:T(8,128)(2,1)} %collective-permute-done.3), kind=kOutput, calls=%fused_computation.5 | convolution fusion | flops 537395200 | bytes 3145728 | tf_op jit(solution)/shard_map/dot_general | solution.py:18
  123.1 1.8 %fusion.52 = f32[512,128]{1,0:T(8,128)S(1)} fusion(f32[512,512]{1,0:T(8,128)S(1)} %fusion.2, f32[512,128]{1,0:T(8,128)S(1)} %copy-done.1), kind=kOutput, calls=%fused_computation.80 | convolution fusion | flops 402653184 | bytes 1572864 | tf_op jit(solution)/shard_map/dot_general | solution.py:25
  124.9 3.9 %collective-permute-start.5 = (f32[512,128]{1,0:T(8,128)S(1)}, f32[512,128]{1,0:T(8,128)S(1)}, u32[]{:S(2)}, u32[]{:S(2)}) collective-permute-start(f32[512,128]{1,0:T(8,128)S(1)} %fusion.52), channel_id=1, source_target_pairs={{0,2},{1,3},{2,4},{3,5},{4,6},{5,7},{6,8},{7,9},{8,10},{9,11},{10,... | collective-permute-start | bytes 786440 | tf_op jit(solution)/shard_map/ppermute | solution.py:10
  128.8 0.6 convolution_bitcast_fusion
  129.4 0.0 collective-permute-done.4
  129.4 1.5 %convolution_multiply_fusion.3 = f32[512,128]{1,0:T(8,128)S(1)} fusion(f32[512,512]{1,0:T(8,128)S(1)} %fusion.2, bf16[512,128]{1,0:T(8,128)(2,1)} %collective-permute-done.4, f32[]{:T(128)S(6)} %convert_element_type.45), kind=kOutput, calls=%fused_computation.7 | convolution fusion | flops 402718720 | bytes 1441796 | tf_op jit(solution)/shard_map/dot_general | solution.py:35
  130.9 0.0 collective-permute-done.1
  130.9 0.0 collective-permute-done.2
  131.0 8.6 %collective-permute-done.5 = f32[512,128]{1,0:T(8,128)S(1)} collective-permute-done((f32[512,128]{1,0:T(8,128)S(1)}, f32[512,128]{1,0:T(8,128)S(1)}, u32[]{:S(2)}, u32[]{:S(2)}) %collective-permute-start.5) | collective-permute-done | bytes 262176 | tf_op jit(solution)/shard_map/ppermute | solution.py:10
  139.6 1.3 fusion.7
  (13 shorter events, 0.1 us)
Async XLA Ops:
  0.0 1.0 copy-start
  0.0 7.6 %copy-start.2 = (f32[1,4,256,256]{3,2,1,0:T(8,128)S(1)}, f32[1,4,256,256]{3,2,1,0:T(8,128)}, u32[]{:S(2)}) copy-start(f32[1,4,256,256]{3,2,1,0:T(8,128)} %param.10) | copy-start | bytes 3145732
  3.0 32.2 %copy-start.1 = (f32[512,128]{1,0:T(8,128)S(1)}, f32[512,128]{1,0:T(8,128)}, u32[]{:S(2)}) copy-start(f32[512,128]{1,0:T(8,128)} %param.8) | copy-start | bytes 786436
  4.4 3.1 %collective-permute-start.7 = (bf16[256,128]{0,1:T(8,128)(2,1)S(1)}, bf16[256,128]{0,1:T(8,128)(2,1)S(1)}, u32[]{:S(2)}, u32[]{:S(2)}) collective-permute-start(bf16[256,128]{0,1:T(8,128)(2,1)S(1)} %get-tuple-element.9), channel_id=1, source_target_pairs={{0,1},{1,0},{2,3},{3,2},{4,5},{5,4},{6,7},{7,6},{8,9},{9,8},{10,11... | collective-permute-start | bytes 196616 | tf_op jit(solution)/shard_map/ppermute | solution.py:14
  7.6 32.9 %copy-start.4 = (f32[256,128]{0,1:T(8,128)}, f32[256,128]{0,1:T(8,128)S(1)}, u32[]{:S(2)}) copy-start(f32[256,128]{0,1:T(8,128)S(1)} %convert_add_fusion.3) | copy-start | bytes 393220
  7.9 6.7 %collective-permute-start.9 = (bf16[256,128]{0,1:T(8,128)(2,1)S(1)}, bf16[256,128]{0,1:T(8,128)(2,1)S(1)}, u32[]{:S(2)}, u32[]{:S(2)}) collective-permute-start(bf16[256,128]{0,1:T(8,128)(2,1)S(1)} %get-tuple-element.11), channel_id=1, source_target_pairs={{0,2},{1,3},{2,0},{3,1},{4,6},{5,7},{6,4},{7,5},{8,10},{9,11},{10,... | collective-permute-start | bytes 196616 | tf_op jit(solution)/shard_map/ppermute | solution.py:14
  14.6 30.8 %copy-start.6 = (f32[256,128]{0,1:T(8,128)}, f32[256,128]{0,1:T(8,128)S(1)}, u32[]{:S(2)}) copy-start(f32[256,128]{0,1:T(8,128)S(1)} %convert_add_fusion.2) | copy-start | bytes 393220
  14.9 25.3 %collective-permute-start.11 = (bf16[256,128]{0,1:T(8,128)(2,1)S(1)}, bf16[256,128]{0,1:T(8,128)(2,1)S(1)}, u32[]{:S(2)}, u32[]{:S(2)}) collective-permute-start(bf16[256,128]{0,1:T(8,128)(2,1)S(1)} %get-tuple-element.13), channel_id=1, source_target_pairs={{0,4},{1,5},{2,6},{3,7},{4,0},{5,1},{6,2},{7,3},{8,12},{9,13},{10,... | collective-permute-start | bytes 196616 | tf_op jit(solution)/shard_map/ppermute | solution.py:14
  21.0 91.8 %collective-permute-start.6 = (f32[256,128]{1,0:T(8,128)S(1)}, f32[256,128]{1,0:T(8,128)}, u32[]{:S(2)}, u32[]{:S(2)}) collective-permute-start(f32[256,128]{1,0:T(8,128)S(1)} %fusion.53), channel_id=1, source_target_pairs={{0,1},{1,0},{2,3},{3,2},{4,5},{5,4},{6,7},{7,6},{8,9},{9,8},{10,11... | collective-permute-start | bytes 393224 | tf_op jit(solution)/shard_map/ppermute | solution.py:14
  22.9 97.9 %collective-permute-start.3 = (bf16[512,1024]{1,0:T(8,128)(2,1)}, bf16[512,1024]{1,0:T(8,128)(2,1)}, u32[]{:S(2)}, u32[]{:S(2)}) collective-permute-start(bf16[512,1024]{1,0:T(8,128)(2,1)} %param.7), channel_id=1, source_target_pairs={{2,0},{3,1},{4,2},{5,3},{6,4},{7,5},{8,6},{9,7},{10,8},{11,9},{12,... | collective-permute-start | bytes 3145736 | tf_op jit(solution)/shard_map/ppermute | solution.py:10
  32.9 81.2 %collective-permute-start = (bf16[512,1024]{1,0:T(8,128)(2,1)}, bf16[512,1024]{1,0:T(8,128)(2,1)}, u32[]{:S(2)}, u32[]{:S(2)}) collective-permute-start(bf16[512,1024]{1,0:T(8,128)(2,1)} %param.7), channel_id=1, source_target_pairs={{1,0},{2,1},{3,2},{4,3},{5,4},{6,5},{7,6},{8,7},{9,8},{10,9},{11,1... | collective-permute-start | bytes 3145736 | tf_op jit(solution)/shard_map/ppermute | solution.py:10
  35.8 93.6 %collective-permute-start.4 = (bf16[512,128]{1,0:T(8,128)(2,1)}, bf16[512,128]{1,0:T(8,128)(2,1)}, u32[]{:S(2)}, u32[]{:S(2)}) collective-permute-start(bf16[512,128]{1,0:T(8,128)(2,1)} %convert_element_type.43), channel_id=1, source_target_pairs={{2,0},{3,1},{4,2},{5,3},{6,4},{7,5},{8,6},{9,7},{10,8},{11,9},{12,... | collective-permute-start | bytes 393224 | tf_op jit(solution)/shard_map/ppermute | solution.py:10
  40.2 0.7 copy-start.7
  40.8 10.1 %collective-permute-start.13 = (bf16[256,128]{0,1:T(8,128)(2,1)S(1)}, bf16[256,128]{0,1:T(8,128)(2,1)S(1)}, u32[]{:S(2)}, u32[]{:S(2)}) collective-permute-start(bf16[256,128]{0,1:T(8,128)(2,1)S(1)} %get-tuple-element.15), channel_id=1, source_target_pairs={{0,8},{1,9},{2,10},{3,11},{4,12},{5,13},{6,14},{7,15},{8,0},{9,1},... | collective-permute-start | bytes 196616 | tf_op jit(solution)/shard_map/ppermute | solution.py:14
  45.3 9.8 %copy-start.8 = (s32[1,4]{1,0:T(1,128)S(1)}, s32[1,4]{1,0:T(1,128)}, u32[]{:S(2)}) copy-start(s32[1,4]{1,0:T(1,128)} %param.12) | copy-start | bytes 52
  45.3 31.1 %copy-start.3 = (f32[1,5,256,256]{3,2,1,0:T(8,128)S(1)}, f32[1,5,256,256]{3,2,1,0:T(8,128)}, u32[]{:S(2)}) copy-start(f32[1,5,256,256]{3,2,1,0:T(8,128)} %param.11) | copy-start | bytes 3932164
  51.6 23.0 %collective-permute-start.14 = (f32[256,128]{0,1:T(8,128)}, f32[256,128]{0,1:T(8,128)}, u32[]{:S(2)}, u32[]{:S(2)}) collective-permute-start(f32[256,128]{0,1:T(8,128)} %convert_add_fusion), channel_id=1, source_target_pairs={{0,16},{1,17},{2,18},{3,19},{4,20},{5,21},{6,22},{7,23},{8,24},{9,... | collective-permute-start | bytes 393224 | tf_op jit(solution)/shard_map/ppermute | solution.py:14
  58.3 35.7 %copy-start.5 = (f32[256,128]{0,1:T(8,128)S(1)}, f32[256,128]{0,1:T(8,128)}, u32[]{:S(2)}) copy-start(f32[256,128]{0,1:T(8,128)} %copy-done.4) | copy-start | bytes 393220
  74.5 11.1 %collective-permute-start.12 = (f32[256,128]{0,1:T(8,128)}, f32[256,128]{0,1:T(8,128)S(1)}, u32[]{:S(2)}, u32[]{:S(2)}) collective-permute-start(f32[256,128]{0,1:T(8,128)} %copy-done.7), channel_id=1, source_target_pairs={{0,8},{1,9},{2,10},{3,11},{4,12},{5,13},{6,14},{7,15},{8,0},{9,1},... | collective-permute-start | bytes 393224 | tf_op jit(solution)/shard_map/ppermute | solution.py:14
  85.6 8.4 %collective-permute-start.10 = (f32[256,128]{0,1:T(8,128)}, f32[256,128]{0,1:T(8,128)S(1)}, u32[]{:S(2)}, u32[]{:S(2)}) collective-permute-start(f32[256,128]{0,1:T(8,128)} %copy-done.6), channel_id=1, source_target_pairs={{0,4},{1,5},{2,6},{3,7},{4,0},{5,1},{6,2},{7,3},{8,12},{9,13},{10,... | collective-permute-start | bytes 393224 | tf_op jit(solution)/shard_map/ppermute | solution.py:14
  94.0 16.0 %collective-permute-start.8 = (f32[256,128]{0,1:T(8,128)S(1)}, f32[256,128]{0,1:T(8,128)S(1)}, u32[]{:S(2)}, u32[]{:S(2)}) collective-permute-start(f32[256,128]{0,1:T(8,128)S(1)} %copy-done.5), channel_id=1, source_target_pairs={{0,2},{1,3},{2,0},{3,1},{4,6},{5,7},{6,4},{7,5},{8,10},{9,11},{10,... | collective-permute-start | bytes 393224 | tf_op jit(solution)/shard_map/ppermute | solution.py:14
  110.0 20.9 %collective-permute-start.1 = (bf16[512,128]{1,0:T(8,128)(2,1)}, bf16[512,128]{1,0:T(8,128)(2,1)S(1)}, u32[]{:S(2)}, u32[]{:S(2)}) collective-permute-start(bf16[512,128]{1,0:T(8,128)(2,1)} %convert_element_type.43), channel_id=1, source_target_pairs={{1,0},{2,1},{3,2},{4,3},{5,4},{6,5},{7,6},{8,7},{9,8},{10,9},{11,1... | collective-permute-start | bytes 393224 | tf_op jit(solution)/shard_map/ppermute | solution.py:10
  118.2 12.8 %collective-permute-start.2 = (f32[512,128]{1,0:T(8,128)S(1)}, f32[512,128]{1,0:T(8,128)S(1)}, u32[]{:S(2)}, u32[]{:S(2)}) collective-permute-start(f32[512,128]{1,0:T(8,128)S(1)} %fusion.51), channel_id=1, source_target_pairs={{0,1},{1,2},{2,3},{3,4},{4,5},{5,6},{6,7},{7,8},{8,9},{9,10},{10,1... | collective-permute-start | bytes 786440 | tf_op jit(solution)/shard_map/ppermute | solution.py:10
  124.9 14.7 %collective-permute-start.5 = (f32[512,128]{1,0:T(8,128)S(1)}, f32[512,128]{1,0:T(8,128)S(1)}, u32[]{:S(2)}, u32[]{:S(2)}) collective-permute-start(f32[512,128]{1,0:T(8,128)S(1)} %fusion.52), channel_id=1, source_target_pairs={{0,2},{1,3},{2,4},{3,5},{4,6},{5,7},{6,8},{7,9},{8,10},{9,11},{10,... | collective-permute-start | bytes 786440 | tf_op jit(solution)/shard_map/ppermute | solution.py:10
where the time goes:
time: 142 us; the launch traced here: 141 us
  starting transfers between devices  59.9 us (42%)
  waiting for transfers between devices  49.2 us (35%)
  matrix products  24.7 us (17%)
  between operations  3.57 us (3%)
  other arithmetic  2.09 us (1%)
  local copies, waits for them, and re-layouts  1.42 us (1%)
    ppermute x9, waiting for transfers between devices, partner(): lax.ppermute(array, axis, [(i, i ^ 1 << distance) for i in range(lax.axis...  40.6 us
    ppermute x9, starting transfers between devices, partner(): lax.ppermute(array, axis, [(i, i ^ 1 << distance) for i in range(lax.axis...  34.9 us
    ppermute x6, starting transfers between devices, from_behind(): return lax.ppermute(array, axis, pairs)  25 us
    dot_general x13, matrix products, apply_matrix(): jnp.dot(matrix, values, precision=lax.Precision.HIGHEST, preferred_elemen...  9.81 us
    ppermute x6, waiting for transfers between devices, from_behind(): return lax.ppermute(array, axis, pairs)  8.62 us
    dot_general x7, matrix products, contract_first(): lax.dot_general(matrix, values, (((0,), (0,)), ((), ())), precision=lax.P...  7.77 us
    dot_general x3, matrix products, kernel_tile(): lax.dot_general(rows_a, rows_b, (((1,), (1,)), ((), ())), preferred_eleme...  7.15 us
  transfers between devices with their start and end apart: 15, of which 8 were waited for; matrix products, arithmetic and copies ran while one was open for 15% of the time, Pallas kernels for 0%

commit v1 on v0

v1 whole, which is shorter than its diff:
```python
import functools

import jax
import jax.numpy as jnp
from jax import lax
from jax.experimental import pallas as pl
from jax.experimental.pallas import tpu as pltpu
from jax.sharding import PartitionSpec as P

F32, BF16 = jnp.float32, jnp.bfloat16
MESH = pl.DeviceIdType.MESH
CHUNKS = 4

NN = (((1,), (0,)), ((), ()))
NT = (((1,), (1,)), ((), ()))
TN = (((0,), (0,)), ((), ()))


def dot(a, b, dims=NN):
    return lax.dot_general(a, b, dims, preferred_element_type=F32)


def split(a):
    high = a.astype(BF16)
    return high, (a - high.astype(F32)).astype(BF16)


def dot3(a, b, dims=NN):
    (ah, al), (bh, bl) = split(a), split(b)
    return dot(ah, bh, dims) + (dot(ah, bl, dims) + dot(al, bh, dims))


def kernel(n, feat, prob, base, tran, coup, nlist, ncount, out,
           phi_q, phi_p, phi_g, phi_o, x_q, x_o, x_cat, x_b, x_p, x_g, u, tm, km,
           s0, s0_r, t1, t1_r, ts, ts_r, ss, ss_r, e1, e1_r, bk, bk_r, acc,
           ld_sem, snd, rcv):
    me = lax.axis_index("leaf")
    core = lax.rem(me, 2)
    rows, feats = phi_q.shape
    ranks = u.shape[1]
    half = x_q.shape[1] // 2
    size = rows // CHUNKS
    g = (3.0 / ranks) ** 0.5
    scale = 1.0 / (feats * rows)
    other = me + 1 - 2 * core
    source = lax.rem(me + n + 2 - 4 * core, n)
    target = lax.rem(me + n - 2 + 4 * core, n)
    sib = [other] + [me + (1 << h) - (2 << h) * lax.rem(me // (1 << h), 2) for h in range(1, 5)]

    def load(src, dst, at):
        copy = pltpu.make_async_copy(src, dst, ld_sem.at[at])
        copy.start()
        return copy

    ld_x = load(prob, x_q, 0)
    ld_u = load(base, u, 1)
    ld_t = load(tran, tm, 2)
    ld_phi = load(feat, phi_q, 3)
    ld_k = load(coup, km, 4)

    barrier = pltpu.get_barrier_semaphore()
    partners = [other, source, target, sib[2], sib[3], sib[4]]
    for p in partners:
        pl.semaphore_signal(barrier, inc=1, device_id=(p,), device_id_type=MESH)
    pl.semaphore_wait(barrier, len(partners))

    count = [0]

    def send(src, dst, to):
        at = count[0]
        count[0] += 1
        copy = pltpu.make_async_remote_copy(
            src_ref=src, dst_ref=dst, send_sem=snd.at[at], recv_sem=rcv.at[at],
            device_id=(to,), device_id_type=MESH)
        copy.start()
        return copy

    def block(k):
        return pl.ds(k * size, size)

    phi_copies = [send(feat.at[block(k)], phi_p.at[block(k)], target) for k in range(CHUNKS)]
    o_copy = send(feat, phi_o, other)
    xo_copy = send(prob, x_o, other)

    ld_x.wait()
    xh, xl = split(x_q[...])
    x_b[...] = xh
    x_copy = send(x_b, x_p, target)
    x_cat[:, :2 * half] = xh
    x_cat[:, 2 * half:] = xl

    ld_u.wait()
    s0[...] = dot3(x_q[...].T, u[...])
    ld_t.wait()
    t1[...] = (g * 2.0 ** -0.5) * dot3(s0[...], tm[0])
    keep = pl.multiple_of(half * core, half)
    give = pl.multiple_of(half - half * core, half)
    t1_copy = send(t1.at[pl.ds(give, half)], t1_r, other)
    s0_copy = send(s0, s0_r, other)

    def member(offset):
        found = jnp.float32(0.0)
        for k in range(nlist.shape[1]):
            hit = jnp.logical_and(nlist[0, k] == me + offset, k < ncount[0])
            found = jnp.maximum(found, jnp.where(hit, 1.0, 0.0))
        return found

    m_p = member(2 - 4 * core)
    m_g = member(2 * core - 1)
    m_o = member(1 - 2 * core)
    m_b = member(4 * core - 2)

    def tile_of(a, b):
        gram = dot(a, b, NT)
        return split(gram * gram * scale)

    def apply_wide(th, tl, cat):
        wide = dot(th, cat)
        return wide[:, :2 * half] + (wide[:, 2 * half:] + dot(tl, cat[:, :2 * half]))

    ld_phi.wait()

    def own(k, carry):
        at = pl.ds(pl.multiple_of(k * 256, 256), 256)
        th, tl = tile_of(phi_q[at, :], phi_q[...])
        acc[at, :] = apply_wide(th, tl, x_cat[...])
        return carry

    lax.fori_loop(0, rows // 256, own, 0)

    def up(level, mine, received):
        s = mine + received
        ss[level - 1] = s.astype(BF16)
        if level == 4:
            return s, None, None, send(ss.at[level - 1], ss_r.at[level - 1], sib[level])
        t = (g * 2.0 ** (-0.5 * (level + 1))) * dot3(s, tm[level])
        ts[level - 1] = t.astype(BF16)
        t_copy = send(ts.at[level - 1], ts_r.at[level - 1], sib[level])
        s_copy = send(ss.at[level - 1], ss_r.at[level - 1], sib[level])
        return s, t, t_copy, s_copy

    t1_copy.wait_recv()
    s1, t2, t2_copy, s1_copy = up(1, t1[pl.ds(keep, half), :], t1_r[...])

    xo_copy.wait_recv()
    o_copy.wait_recv()
    xoh, xol = split(x_o[...])
    xo_cat = jnp.concatenate([xoh, xol], axis=1)

    def beside(k, carry):
        at = pl.ds(pl.multiple_of(k * 256, 256), 256)
        th, tl = tile_of(phi_q[at, :], phi_o[...])
        acc[at, :] += m_o * apply_wide(th, tl, xo_cat)
        return carry

    lax.fori_loop(0, rows // 256, beside, 0)

    t2_copy.wait_recv()
    s2, t3, t3_copy, s2_copy = up(2, t2, ts_r[0].astype(F32))

    fwd, back = [], []
    x_copy.wait_recv()
    xg_copy = send(x_p, x_g, other)

    def far_pair(k):
        phi_copies[k].wait_recv()
        fwd.append(send(phi_p.at[block(k)], phi_g.at[block(k)], other))
        th, tl = tile_of(phi_p[block(k), :], phi_q[...])
        bk[block(k), :] = apply_wide(th, tl, x_cat[...]).astype(BF16)
        back.append(send(bk.at[block(k)], bk_r.at[block(k)], source))
        xs = x_p[block(k), :]
        acc[...] += m_p * (dot(th, xs, TN) + dot(tl, xs, TN))

    def near_pair(k):
        fwd[k].wait_recv()
        th, tl = tile_of(phi_q[...], phi_g[block(k), :])
        xs = x_g[block(k), :]
        acc[...] += m_g * (dot(th, xs) + dot(tl, xs))

    far_pair(0)
    t3_copy.wait_recv()
    s3, t4, t4_copy, s3_copy = up(3, t3, ts_r[1].astype(F32))
    xg_copy.wait_recv()
    far_pair(1)
    near_pair(0)
    t4_copy.wait_recv()
    _, _, _, s4_copy = up(4, t4, ts_r[2].astype(F32))
    far_pair(2)
    near_pair(1)

    ld_k.wait()
    s0_copy.wait_recv()
    c0 = g * dot3(s0_r[...], km[0], NT)
    coupled = []
    for level, copy in ((1, s1_copy), (2, s2_copy), (3, s3_copy), (4, s4_copy)):
        copy.wait_recv()
        received = ss_r[level - 1]
        kh, kl = split(km[level])
        coupled.append(g * (dot(received, kh, NT) + dot(received, kl, NT)))
    e = coupled[3]
    for level in (3, 2, 1):
        e = coupled[level - 1] + (g * 2.0 ** (-0.5 * (level + 1))) * dot3(e, tm[level], NT)
    e1[...] = e
    e1_copy = send(e1, e1_r, other)
    far_pair(3)
    near_pair(2)
    e1_copy.wait_recv()
    mine, theirs = e1[...], e1_r[...]
    first = jnp.where(core == 0, mine, theirs)
    second = jnp.where(core == 0, theirs, mine)
    e0 = c0 + (g * 2.0 ** -0.5) * dot3(jnp.concatenate([first, second], axis=0), tm[0], NT)
    acc[...] += dot3(u[...], e0, NT)
    near_pair(3)
    for copy in back:
        copy.wait_recv()
    out[...] = acc[...] + m_b * bk_r[...].astype(F32)

    sent = phi_copies + [o_copy, xo_copy, x_copy, t1_copy, s0_copy, t2_copy, s1_copy, t3_copy, s2_copy, xg_copy]
    sent += fwd + back + [t4_copy, s3_copy, s4_copy, e1_copy]
    for copy in sent:
        copy.wait_send()


def shards(n, features, probes, bases, transfers, couplings, near_list, near_count):
    rows, feats = features.shape
    width = probes.shape[1]
    half = width // 2
    ranks = bases.shape[1]
    levels = transfers.shape[1]
    sends = 3 * CHUNKS + 14
    hbm = pl.BlockSpec(memory_space=pltpu.HBM)
    smem = pl.BlockSpec(memory_space=pltpu.SMEM)

    def vmem(*shape, dtype=F32):
        return pltpu.VMEM(shape, dtype)

    return pl.pallas_call(
        functools.partial(kernel, n),
        out_shape=jax.ShapeDtypeStruct((rows, width), F32),
        in_specs=[hbm] * 5 + [smem] * 2,
        out_specs=pl.BlockSpec(memory_space=pltpu.VMEM),
        scratch_shapes=[
            vmem(rows, feats, dtype=BF16), vmem(rows, feats, dtype=BF16),
            vmem(rows, feats, dtype=BF16), vmem(rows, feats, dtype=BF16),
            vmem(rows, width), vmem(rows, width),
            vmem(rows, 2 * width, dtype=BF16), vmem(rows, width, dtype=BF16),
            vmem(rows, width, dtype=BF16), vmem(rows, width, dtype=BF16),
            vmem(rows, ranks), vmem(levels, ranks, ranks), vmem(levels + 1, ranks, ranks),
            vmem(width, ranks), vmem(width, ranks), vmem(width, ranks), vmem(half, ranks),
            vmem(3, half, ranks, dtype=BF16), vmem(3, half, ranks, dtype=BF16),
            vmem(4, half, ranks, dtype=BF16), vmem(4, half, ranks, dtype=BF16),
            vmem(half, ranks), vmem(half, ranks),
            vmem(rows, width, dtype=BF16), vmem(rows, width, dtype=BF16),
            vmem(rows, width),
            pltpu.SemaphoreType.DMA((5,)),
            pltpu.SemaphoreType.DMA((sends,)),
            pltpu.SemaphoreType.DMA((sends,)),
        ],
        compiler_params=pltpu.CompilerParams(
            collective_id=0, has_side_effects=True, vmem_limit_bytes=56 * 1024 * 1024),
    )(features, probes, bases, transfers[0], couplings[0], near_list, near_count)


def solution(mesh):
    in_specs = (
        P("leaf", None),
        P("leaf", None),
        P("leaf", None),
        P("leaf", None, None, None),
        P("leaf", None, None, None),
        P("leaf", None),
        P("leaf"),
    )
    return jax.shard_map(
        functools.partial(shards, mesh.shape["leaf"]),
        mesh=mesh, in_specs=in_specs, out_specs=P("leaf", None), check_vma=False)
```

time: 142 us -> 47.7 us (0.34)
  starting transfers between devices: 59.9 us -> 0 us
  waiting for transfers between devices: 49.2 us -> 0 us
  Pallas kernels: 0 us -> 45.2 us
  matrix products: 24.7 us -> 0 us
  between operations: 3.57 us -> 0.66 us
  other arithmetic: 2.09 us -> 0 us
    ppermute x15 -> x0, starting transfers between devices: 59.9 us -> none  [the longest x9 34.9 us: partner(): lax.ppermute(array, axis, [(i, i ^ 1 << distance) for i in range(lax.axis...]
    ppermute x15 -> x0, waiting for transfers between devices: 49.2 us -> none  [the longest x9 40.6 us: partner(): lax.ppermute(array, axis, [(i, i ^ 1 << distance) for i in range(lax.axis...]
    pallas_call x0 -> x1, Pallas kernels: none -> 45.2 us  [shards(): pl.pallas_call(functools.partial(kernel, n), out_shape=jax.ShapeDtypeStru...]
    dot_general x23 -> x0, matrix products: 24.7 us -> none  [the longest x13 9.81 us: apply_matrix(): jnp.dot(matrix, values, precision=lax.Precision.HIGHEST, preferred_elemen...]
  transfers between devices with their start and end apart: 15 -> 0, of which waited for: 8 -> 0; matrix products, arithmetic and copies ran while one was open for 15% -> 0% of each run, Pallas kernels for 0% -> 0%
where the time goes in v1:
time: 47.7 us; the launch traced here: 47.5 us
  Pallas kernels  45.2 us (95%)
  local copies, waits for them, and re-layouts  1.67 us (4%)
  between operations  0.66 us (1%)
    pallas_call x1, Pallas kernels, shards(): pl.pallas_call(functools.partial(kernel, n), out_shape=jax.ShapeDtypeStru...  45.2 us
    unnamed x1, local copies, waits for them, and re-layouts  1.67 us

profile of v1, /device:TPU:6, one launch (start us, length us, event | category | flops | bytes accessed | tf_op | source)
XLA Modules:
  0.0 47.5 jit_solution(11802367159433543395)
XLA Ops:
  0.7 45.2 %shard_map.73 = f32[512,128]{1,0:T(8,128)} custom-call(bf16[512,1024]{1,0:T(8,128)(2,1)} %feat.1, f32[512,128]{1,0:T(8,128)} %prob.1, f32[512,256]{1,0:T(8,128)} %base.1, f32[4,256,256]{2,1,0:T(8,128)} %bitcast.3, f32[5,256,256]{2,1,0:T(8,128)} %bitcast.2, s32[1,4]{1,0:T(1,128)} %nlist.1, s32[1]{0:T(128)S(6)} %copy.9.ncount), custom_call_target="tpu_custom_call" | custom-call | tf_op jit(solution)/shard_map/pallas_call | solution.py:237
  45.9 1.7 %copy.10 = f32[512,128]{1,0:T(8,128)} copy(f32[512,128]{1,0:T(8,128)} %shard_map.73) | data formatting | bytes 524288

commit v2 on v1

v2 whole, which is shorter than its diff:
```python
import functools

import jax
import jax.numpy as jnp
from jax import lax
from jax.experimental import pallas as pl
from jax.experimental.pallas import tpu as pltpu
from jax.sharding import PartitionSpec as P

F32, BF16 = jnp.float32, jnp.bfloat16
MESH = pl.DeviceIdType.MESH
CHUNKS = 16
BLOCKS = 4
DEPTH = 3

NN = (((1,), (0,)), ((), ()))
NT = (((1,), (1,)), ((), ()))
TN = (((0,), (0,)), ((), ()))


def dot(a, b, dims=NN):
    return lax.dot_general(a, b, dims, preferred_element_type=F32)


def split(a):
    high = a.astype(BF16)
    return high, (a - high.astype(F32)).astype(BF16)


def dot3(a, b, dims=NN):
    (ah, al), (bh, bl) = split(a), split(b)
    return dot(ah, bh, dims) + (dot(ah, bl, dims) + dot(al, bh, dims))


class Move:
    def __init__(self, copy, sends=None, receives=None):
        self.copy, self.sends, self.receives = copy, sends, receives

    @staticmethod
    def run(act, when):
        if when is None:
            act()
        else:
            pl.when(when)(act)

    def start(self):
        self.run(self.copy.start, self.sends)
        return self

    def wait_send(self):
        self.run(self.copy.wait_send, self.sends)

    def wait_recv(self):
        self.run(self.copy.wait_recv, self.receives)


def kernel(n, feat, prob, base, tran, coup, nlist, ncount, out,
           phi_q, phi_p, phi_g, phi_o, x_q, x_o, x_cat, x_b, x_p, x_g, u, tm, km,
           s0, s0_r, t1, t1_r, ts, ts_r, ss, ss_r, e1, e1_r, bk, bk_r, acc,
           ld_sem, snd, rcv):
    me = lax.axis_index("leaf")
    core = lax.rem(me, 2)
    rows, feats = phi_q.shape
    ranks = u.shape[1]
    half = x_q.shape[1] // 2
    g = (3.0 / ranks) ** 0.5
    scale = 1.0 / (feats * rows)

    def flip(h):
        return (1 << h) - (2 << h) * lax.rem(me // (1 << h), 2)

    other = me + flip(0)
    source = me + 2 - 4 * core
    target = me - 2 + 4 * core
    has_source = jnp.logical_and(source >= 0, source < n)
    has_target = jnp.logical_and(target >= 0, target < n)
    sib = [other, me + flip(1), me + flip(2), me + flip(2) + flip(3), me + flip(4)]

    def load(src, dst, at):
        copy = pltpu.make_async_copy(src, dst, ld_sem.at[at])
        copy.start()
        return copy

    ld_x = load(prob, x_q, 0)
    ld_u = load(base, u, 1)
    ld_t = load(tran, tm, 2)
    ld_phi = load(feat, phi_q, 3)
    ld_k = load(coup, km, 4)

    barrier = pltpu.get_barrier_semaphore()

    def greet(p):
        pl.semaphore_signal(barrier, inc=1, device_id=(p,), device_id_type=MESH)

    for p in (other, sib[2], sib[3], sib[4]):
        greet(p)
    pl.when(has_source)(lambda: greet(source))
    pl.when(has_target)(lambda: greet(target))
    pl.semaphore_wait(barrier, 4 + has_source.astype(jnp.int32) + has_target.astype(jnp.int32))

    count, sent = [0], []

    def move(src, dst, to, sends=None, receives=None):
        at = count[0]
        count[0] += 1
        return Move(pltpu.make_async_remote_copy(
            src_ref=src, dst_ref=dst, send_sem=snd.at[at], recv_sem=rcv.at[at],
            device_id=(to,), device_id_type=MESH), sends, receives)

    def send(*args):
        sent.append(move(*args).start())
        return sent[-1]

    def ahead(src, dst):
        return move(src, dst, target, has_target, has_source)

    def part(k, parts):
        return pl.ds(k * (rows // parts), rows // parts)

    phi_moves = [ahead(feat.at[part(k, CHUNKS)], phi_p.at[part(k, CHUNKS)]) for k in range(CHUNKS)]
    x_moves = [ahead(x_b.at[part(k, 2)], x_p.at[part(k, 2)]) for k in range(2)]
    waiting = phi_moves[:5] + x_moves + phi_moves[5:]
    flying = []

    def pump(times=1):
        for _ in range(times):
            if waiting:
                if len(flying) == DEPTH:
                    flying.pop(0).wait_send()
                flying.append(waiting.pop(0).start())

    pump(DEPTH)
    o_moves = [send(feat.at[part(k, 2)], phi_o.at[part(k, 2)], other) for k in range(2)]
    xo_move = send(prob, x_o, other)

    @pl.when(jnp.logical_not(has_source))
    def _():
        phi_p[...] = jnp.zeros_like(phi_p)
        x_p[...] = jnp.zeros_like(x_p)

    @pl.when(jnp.logical_not(has_target))
    def _():
        bk_r[...] = jnp.zeros_like(bk_r)

    ld_x.wait()
    xh, xl = split(x_q[...])
    x_b[...] = xh
    x_cat[:, :2 * half] = xh
    x_cat[:, 2 * half:] = xl

    ld_u.wait()
    s0[...] = dot3(x_q[...].T, u[...])
    ld_t.wait()
    t1[...] = (g * 2.0 ** -0.5) * dot3(s0[...], tm[0])
    keep = pl.multiple_of(half * core, half)
    give = pl.multiple_of(half - half * core, half)
    t1_move = send(t1.at[pl.ds(give, half)], t1_r, other)
    s0_move = send(s0, s0_r, other)
    pump()

    def member(offset):
        found = jnp.float32(0.0)
        for k in range(nlist.shape[1]):
            hit = jnp.logical_and(nlist[0, k] == me + offset, k < ncount[0])
            found = jnp.maximum(found, jnp.where(hit, 1.0, 0.0))
        return found

    m_p = member(2 - 4 * core)
    m_g = member(2 * core - 1)
    m_o = member(1 - 2 * core)
    m_b = member(4 * core - 2)

    def tile_of(a, b):
        gram = dot(a, b, NT)
        return split(gram * gram * scale)

    def apply_wide(th, tl, cat):
        wide = dot(th, cat)
        return wide[:, :2 * half] + (wide[:, 2 * half:] + dot(tl, cat[:, :2 * half]))

    def own(k):
        th, tl = tile_of(phi_q[part(k, 2), :], phi_q[...])
        acc[part(k, 2), :] = apply_wide(th, tl, x_cat[...])

    def beside(k):
        if k == 0:
            xo_move.wait_recv()
        o_moves[k].wait_recv()
        th, tl = tile_of(phi_q[...], phi_o[part(k, 2), :])
        xoh, xol = split(x_o[part(k, 2), :])
        acc[...] += m_o * apply_wide(th, tl, jnp.concatenate([xoh, xol], axis=1))

    def up(level, mine, received):
        s = mine + received
        ss[level - 1] = s.astype(BF16)
        if level == 4:
            return None, None, send(ss.at[level - 1], ss_r.at[level - 1], sib[level])
        t = (g * 2.0 ** (-0.5 * (level + 1))) * dot3(s, tm[level])
        ts[level - 1] = t.astype(BF16)
        t_move = send(ts.at[level - 1], ts_r.at[level - 1], sib[level])
        s_move = send(ss.at[level - 1], ss_r.at[level - 1], sib[level])
        return t, t_move, s_move

    fwd, back = [], []

    def far_pair(k):
        if k == 0:
            for m in x_moves:
                m.wait_recv()
            fwd.append(send(x_p, x_g, other))
        for m in phi_moves[k * CHUNKS // BLOCKS:(k + 1) * CHUNKS // BLOCKS]:
            m.wait_recv()
        at = part(k, BLOCKS)
        fwd.append(send(phi_p.at[at], phi_g.at[at], other))
        th, tl = tile_of(phi_p[at, :], phi_q[...])
        bk[at, :] = apply_wide(th, tl, x_cat[...]).astype(BF16)
        back.append(send(bk.at[at], bk_r.at[at], source, has_source, has_target))
        xs = x_p[at, :]
        acc[...] += m_p * (dot(th, xs, TN) + dot(tl, xs, TN))

    def near_pair(k):
        if k == 0:
            fwd[0].wait_recv()
        fwd[k + 1].wait_recv()
        at = part(k, BLOCKS)
        th, tl = tile_of(phi_q[...], phi_g[at, :])
        xs = x_g[at, :]
        acc[...] += m_g * (dot(th, xs) + dot(tl, xs))

    coupled = [None] * 5

    def couple(level, move):
        move.wait_recv()
        if level == 0:
            coupled[0] = g * dot3(s0_r[...], km[0], NT)
        else:
            received = ss_r[level - 1]
            kh, kl = split(km[level])
            coupled[level] = g * (dot(received, kh, NT) + dot(received, kl, NT))

    ld_phi.wait()
    own(0)
    pump()
    t1_move.wait_recv()
    t2, t2_move, s1_move = up(1, t1[pl.ds(keep, half), :], t1_r[...])
    pump()
    own(1)
    pump()
    beside(0)
    pump()
    t2_move.wait_recv()
    t3, t3_move, s2_move = up(2, t2, ts_r[0].astype(F32))
    pump()
    beside(1)
    pump()
    ld_k.wait()
    couple(0, s0_move)
    pump()
    t3_move.wait_recv()
    t4, t4_move, s3_move = up(3, t3, ts_r[1].astype(F32))
    pump()
    far_pair(0)
    pump()
    couple(1, s1_move)
    pump()
    t4_move.wait_recv()
    _, _, s4_move = up(4, t4, ts_r[2].astype(F32))
    pump()
    far_pair(1)
    pump()
    near_pair(0)
    pump()
    couple(2, s2_move)
    couple(3, s3_move)
    pump(2)
    far_pair(2)
    pump(len(waiting))
    couple(4, s4_move)
    e = coupled[4]
    for level in (3, 2, 1):
        e = coupled[level] + (g * 2.0 ** (-0.5 * (level + 1))) * dot3(e, tm[level], NT)
    e1[...] = e
    e1_move = send(e1, e1_r, other)
    near_pair(1)
    far_pair(3)
    near_pair(2)
    e1_move.wait_recv()
    mine, theirs = e1[...], e1_r[...]
    first = jnp.where(core == 0, mine, theirs)
    second = jnp.where(core == 0, theirs, mine)
    e0 = coupled[0] + (g * 2.0 ** -0.5) * dot3(jnp.concatenate([first, second], axis=0), tm[0], NT)
    acc[...] += dot3(u[...], e0, NT)
    near_pair(3)
    for m in back:
        m.wait_recv()
    out[...] = acc[...] + m_b * bk_r[...].astype(F32)
    for m in flying + sent:
        m.wait_send()


def shards(n, features, probes, bases, transfers, couplings, near_list, near_count):
    rows, feats = features.shape
    width = probes.shape[1]
    half = width // 2
    ranks = bases.shape[1]
    levels = transfers.shape[1]
    sends = CHUNKS + 2 * BLOCKS + 17
    hbm = pl.BlockSpec(memory_space=pltpu.HBM)
    smem = pl.BlockSpec(memory_space=pltpu.SMEM)

    def vmem(*shape, dtype=F32):
        return pltpu.VMEM(shape, dtype)

    return pl.pallas_call(
        functools.partial(kernel, n),
        out_shape=jax.ShapeDtypeStruct((rows, width), F32),
        in_specs=[hbm] * 5 + [smem] * 2,
        out_specs=pl.BlockSpec(memory_space=pltpu.VMEM),
        scratch_shapes=[
            vmem(rows, feats, dtype=BF16), vmem(rows, feats, dtype=BF16),
            vmem(rows, feats, dtype=BF16), vmem(rows, feats, dtype=BF16),
            vmem(rows, width), vmem(rows, width),
            vmem(rows, 2 * width, dtype=BF16), vmem(rows, width, dtype=BF16),
            vmem(rows, width, dtype=BF16), vmem(rows, width, dtype=BF16),
            vmem(rows, ranks), vmem(levels, ranks, ranks), vmem(levels + 1, ranks, ranks),
            vmem(width, ranks), vmem(width, ranks), vmem(width, ranks), vmem(half, ranks),
            vmem(3, half, ranks, dtype=BF16), vmem(3, half, ranks, dtype=BF16),
            vmem(4, half, ranks, dtype=BF16), vmem(4, half, ranks, dtype=BF16),
            vmem(half, ranks), vmem(half, ranks),
            vmem(rows, width, dtype=BF16), vmem(rows, width, dtype=BF16),
            vmem(rows, width),
            pltpu.SemaphoreType.DMA((5,)),
            pltpu.SemaphoreType.DMA((sends,)),
            pltpu.SemaphoreType.DMA((sends,)),
        ],
        compiler_params=pltpu.CompilerParams(
            collective_id=0, has_side_effects=True, vmem_limit_bytes=56 * 1024 * 1024),
    )(features, probes, bases, transfers[0], couplings[0], near_list, near_count)


def solution(mesh):
    in_specs = (
        P("leaf", None),
        P("leaf", None),
        P("leaf", None),
        P("leaf", None, None, None),
        P("leaf", None, None, None),
        P("leaf", None),
        P("leaf"),
    )
    return jax.shard_map(
        functools.partial(shards, mesh.shape["leaf"]),
        mesh=mesh, in_specs=in_specs, out_specs=P("leaf", None), check_vma=False)
```

time: 47.7 us -> 45 us (0.943)
  Pallas kernels: 45.2 us -> 42.1 us
    pallas_call x1, Pallas kernels: 45.2 us -> 42.1 us  [shards(): pl.pallas_call(functools.partial(kernel, n), out_shape=jax.ShapeDtypeStru...]
where the time goes in v2:
time: 45 us; the launch traced here: 44.4 us
  Pallas kernels  42.1 us (94%)
  local copies, waits for them, and re-layouts  1.67 us (4%)
  between operations  0.66 us (1%)
    pallas_call x1, Pallas kernels, shards(): pl.pallas_call(functools.partial(kernel, n), out_shape=jax.ShapeDtypeStru...  42.1 us
    unnamed x1, local copies, waits for them, and re-layouts  1.67 us

profile of v2, /device:TPU:6, one launch (start us, length us, event | category | flops | bytes accessed | tf_op | source)
XLA Modules:
  0.0 44.4 jit_solution(8220835816377420904)
XLA Ops:
  0.7 42.1 %shard_map.73 = f32[512,128]{1,0:T(8,128)} custom-call(bf16[512,1024]{1,0:T(8,128)(2,1)} %feat.1, f32[512,128]{1,0:T(8,128)} %prob.1, f32[512,256]{1,0:T(8,128)} %base.1, f32[4,256,256]{2,1,0:T(8,128)} %bitcast.3, f32[5,256,256]{2,1,0:T(8,128)} %bitcast.2, s32[1,4]{1,0:T(1,128)} %nlist.1, s32[1]{0:T(128)S(6)} %copy.9.ncount), custom_call_target="tpu_custom_call" | custom-call | tf_op jit(solution)/shard_map/pallas_call | solution.py:314
  42.7 1.7 %copy.10 = f32[512,128]{1,0:T(8,128)} copy(f32[512,128]{1,0:T(8,128)} %shard_map.73) | data formatting | bytes 524288

commit v3 on v2

v3 whole, which is shorter than its diff:
```python
import functools

import jax
import jax.numpy as jnp
from jax import lax
from jax.experimental import pallas as pl
from jax.experimental.pallas import tpu as pltpu
from jax.sharding import PartitionSpec as P

F32, BF16 = jnp.float32, jnp.bfloat16
MESH = pl.DeviceIdType.MESH
CHUNKS = 16
BLOCKS = ((0, 256), (256, 128), (384, 128))
BURSTS = (5, 6, 7)

NN = (((1,), (0,)), ((), ()))
NT = (((1,), (1,)), ((), ()))
TN = (((0,), (0,)), ((), ()))


def dot(a, b, dims=NN):
    return lax.dot_general(a, b, dims, preferred_element_type=F32)


def split(a):
    high = a.astype(BF16)
    return high, (a - high.astype(F32)).astype(BF16)


def dot3(a, b, dims=NN):
    (ah, al), (bh, bl) = split(a), split(b)
    return dot(ah, bh, dims) + (dot(ah, bl, dims) + dot(al, bh, dims))


class Move:
    def __init__(self, copy, sends=None, receives=None):
        self.copy, self.sends, self.receives = copy, sends, receives

    @staticmethod
    def run(act, when):
        if when is None:
            act()
        else:
            pl.when(when)(act)

    def start(self):
        self.run(self.copy.start, self.sends)
        return self

    def wait_send(self):
        self.run(self.copy.wait_send, self.sends)

    def wait_recv(self):
        self.run(self.copy.wait_recv, self.receives)


def kernel(n, feat, prob, base, tran, coup, nlist_hbm, ncount_hbm, out,
           phi_q, phi_p, phi_g, phi_o, x_q, x_o, x_cat, x_b, x_p, x_g, u, tm, km,
           s0, s0_r, t1, t1_r, t2, t2_r, v3, v3_r, t4, ss, ss_r, e1, e1_r, bk, bk_r, acc,
           nlist, ncount, ld_sem, snd, rcv):
    me = lax.axis_index("leaf")
    core = lax.rem(me, 2)
    rows, feats = phi_q.shape
    ranks = u.shape[1]
    half = x_q.shape[1] // 2
    g = (3.0 / ranks) ** 0.5
    scale = 1.0 / (feats * rows)

    def flip(h):
        return (1 << h) - (2 << h) * lax.rem(me // (1 << h), 2)

    other = me + flip(0)
    source = me + 2 - 4 * core
    target = me - 2 + 4 * core
    has_source = jnp.logical_and(source >= 0, source < n)
    has_target = jnp.logical_and(target >= 0, target < n)
    next_chip, cross, cross_next = me + flip(1), me + flip(2), me + flip(1) + flip(2)
    level3 = me + flip(2) + flip(3)
    level4, level4_far = me + flip(4), me + flip(2) + flip(3) + flip(4)
    early = lax.rem(me // 2, 8) < 4
    late = jnp.logical_not(early)

    barrier = pltpu.get_barrier_semaphore()

    def greet(p):
        pl.semaphore_signal(barrier, inc=1, device_id=(p,), device_id_type=MESH)

    fixed = (other, cross_next, level4_far, level3, cross, level4)
    pl.when(has_target)(lambda: greet(target))
    pl.when(has_source)(lambda: greet(source))
    for p in fixed:
        greet(p)

    def load(src, dst, at):
        copy = pltpu.make_async_copy(src, dst, ld_sem.at[at])
        copy.start()
        return copy

    ld_x = load(prob, x_q, 0)
    ld_u = load(base, u, 1)
    ld_t = load(tran, tm, 2)
    ld_phi = load(feat, phi_q, 3)
    ld_k = load(coup, km, 4)
    ld_list = load(nlist_hbm, nlist, 5)
    ld_count = load(ncount_hbm, ncount, 6)

    def member(offset):
        found = jnp.float32(0.0)
        for k in range(nlist.shape[1]):
            hit = jnp.logical_and(nlist[0, k] == me + offset, k < ncount[0])
            found = jnp.maximum(found, jnp.where(hit, 1.0, 0.0))
        return found

    def tile_of(a, b):
        gram = dot(a, b, NT)
        return split(gram * gram * scale)

    def apply_wide(th, tl, cat):
        wide = dot(th, cat)
        return wide[:, :2 * half] + (wide[:, 2 * half:] + dot(tl, cat[:, :2 * half]))

    def split_probes():
        ld_x.wait()
        xh, xl = split(x_q[...])
        x_b[...] = xh
        x_cat[:, :2 * half] = xh
        x_cat[:, 2 * half:] = xl

    def own():
        def step(k, carry):
            at = pl.ds(pl.multiple_of(k * 256, 256), 256)
            th, tl = tile_of(phi_q[at, :], phi_q[...])
            acc[at, :] += apply_wide(th, tl, x_cat[...])
            return carry

        lax.fori_loop(0, rows // 256, step, 0)

    acc[...] = jnp.zeros_like(acc)

    @pl.when(early)
    def _():
        split_probes()
        for ld in (ld_u, ld_t, ld_phi, ld_k):
            ld.wait()
        own()

    pl.semaphore_wait(barrier, len(fixed) + has_source.astype(jnp.int32) + has_target.astype(jnp.int32))

    count, sent = [0], []

    def move(src, dst, to, sends=None, receives=None):
        at = count[0]
        count[0] += 1
        return Move(pltpu.make_async_remote_copy(
            src_ref=src, dst_ref=dst, send_sem=snd.at[at], recv_sem=rcv.at[at],
            device_id=(to,), device_id_type=MESH), sends, receives)

    def send(*args):
        sent.append(move(*args).start())
        return sent[-1]

    def ahead(src, dst):
        return move(src, dst, target, has_target, has_source)

    def part(k, parts):
        return pl.ds(k * (rows // parts), rows // parts)

    phi_moves = [ahead(feat.at[part(k, CHUNKS)], phi_p.at[part(k, CHUNKS)]) for k in range(CHUNKS)]
    x_moves = [ahead(x_b.at[part(k, 2)], x_p.at[part(k, 2)]) for k in range(2)]
    waiting = phi_moves[:6] + x_moves + phi_moves[6:]

    def burst(times):
        for _ in range(times):
            waiting.pop(0).start()

    burst(BURSTS[0])
    o_moves = [send(feat.at[part(k, 2)], phi_o.at[part(k, 2)], other) for k in range(2)]
    xo_move = send(prob, x_o, other)

    @pl.when(jnp.logical_not(has_source))
    def _():
        phi_p[...] = jnp.zeros_like(phi_p)
        x_p[...] = jnp.zeros_like(x_p)

    @pl.when(jnp.logical_not(has_target))
    def _():
        bk_r[...] = jnp.zeros_like(bk_r)

    pl.when(late)(split_probes)

    pl.when(late)(ld_u.wait)
    s0[...] = dot3(x_q[...].T, u[...])
    pl.when(late)(ld_t.wait)
    t1[...] = (g * 2.0 ** -0.5) * dot3(s0[...], tm[0])
    keep = pl.multiple_of(half * core, half)
    give = pl.multiple_of(half - half * core, half)
    t1_move = send(t1.at[pl.ds(give, half)], t1_r, other)
    s0_move = send(s0, s0_r, other)

    ld_list.wait()
    ld_count.wait()
    m_p = member(2 - 4 * core)
    m_g = member(2 * core - 1)
    m_o = member(1 - 2 * core)
    m_b = member(4 * core - 2)

    def beside(k):
        if k == 0:
            xo_move.wait_recv()
        o_moves[k].wait_recv()
        th, tl = tile_of(phi_q[...], phi_o[part(k, 2), :])
        xoh, xol = split(x_o[part(k, 2), :])
        acc[...] += m_o * apply_wide(th, tl, jnp.concatenate([xoh, xol], axis=1))

    fwd, back = [], []

    def far_pair(k):
        start, length = BLOCKS[k]
        at = pl.ds(start, length)
        if k == 0:
            for m in x_moves:
                m.wait_recv()
            fwd.append(send(x_p, x_g, other))
        for m in phi_moves[start * CHUNKS // rows:(start + length) * CHUNKS // rows]:
            m.wait_recv()
        fwd.append(send(phi_p.at[at], phi_g.at[at], other))
        th, tl = tile_of(phi_p[at, :], phi_q[...])
        bk[at, :] = apply_wide(th, tl, x_cat[...]).astype(BF16)
        back.append(send(bk.at[at], bk_r.at[at], source, has_source, has_target))
        xs = x_p[at, :]
        acc[...] += m_p * (dot(th, xs, TN) + dot(tl, xs, TN))

    def near_pair(k):
        start, length = BLOCKS[k]
        at = pl.ds(start, length)
        if k == 0:
            fwd[0].wait_recv()
        fwd[k + 1].wait_recv()
        th, tl = tile_of(phi_q[...], phi_g[at, :])
        xs = x_g[at, :]
        acc[...] += m_g * (dot(th, xs) + dot(tl, xs))

    def factor(level):
        return g * 2.0 ** (-0.5 * level)

    t1_move.wait_recv()
    s1 = t1[pl.ds(keep, half), :] + t1_r[...]
    mine2 = factor(2) * dot3(s1, tm[1])
    t2[...] = mine2.astype(BF16)
    t2_move = send(t2, t2_r, next_chip)
    mine3 = factor(3) * dot3(mine2, tm[2])
    v3[...] = mine3.astype(BF16)
    v3_moves = [send(v3, v3_r.at[1], cross_next), send(v3, v3_r.at[0], cross)]
    ss[0] = s1.astype(BF16)
    s1_move = send(ss.at[0], ss_r.at[0], next_chip)
    burst(BURSTS[1])
    pl.when(late)(ld_phi.wait)
    beside(0)
    beside(1)

    t2_move.wait_recv()
    from2 = t2_r[...]
    ss[1] = (mine2 + from2.astype(F32)).astype(BF16)
    s2_move = send(ss.at[1], ss_r.at[1], cross)
    t2h, t2l = split(tm[2])
    mine3 = mine3 + factor(3) * (dot(from2, t2h) + dot(from2, t2l))
    pl.when(late)(ld_k.wait)
    s0_move.wait_recv()
    e0 = g * dot3(s0_r[...], km[0], NT)
    for m in v3_moves:
        m.wait_recv()
    s3 = mine3 + (v3_r[0].astype(F32) + v3_r[1].astype(F32))
    t4[...] = (factor(4) * dot3(s3, tm[3])).astype(BF16)
    t4_moves = [send(t4, ss_r.at[4], level4_far), send(t4, ss_r.at[3], level4)]
    ss[2] = s3.astype(BF16)
    s3_move = send(ss.at[2], ss_r.at[2], level3)
    burst(BURSTS[2])

    def couple(level, m):
        m.wait_recv()
        received = ss_r[level - 1]
        kh, kl = split(km[level])
        return g * (dot(received, kh, NT) + dot(received, kl, NT))

    coupled1 = couple(1, s1_move)
    far_pair(0)
    near_pair(0)
    coupled2 = couple(2, s2_move)
    far_pair(1)
    for m in t4_moves:
        m.wait_recv()
    e = g * dot3(ss_r[3].astype(F32) + ss_r[4].astype(F32), km[4], NT)
    e = couple(3, s3_move) + factor(4) * dot3(e, tm[3], NT)
    e = coupled2 + factor(3) * dot3(e, tm[2], NT)
    e1[...] = coupled1 + factor(2) * dot3(e, tm[1], NT)
    e1_move = send(e1, e1_r, other)
    near_pair(1)
    far_pair(2)
    e1_move.wait_recv()
    mine, theirs = e1[...], e1_r[...]
    first = jnp.where(core == 0, mine, theirs)
    second = jnp.where(core == 0, theirs, mine)
    e0 = e0 + factor(1) * dot3(jnp.concatenate([first, second], axis=0), tm[0], NT)
    acc[...] += dot3(u[...], e0, NT)
    near_pair(2)
    pl.when(late)(own)
    for m in back:
        m.wait_recv()
    out[...] = acc[...] + m_b * bk_r[...].astype(F32)
    for m in phi_moves + x_moves + sent:
        m.wait_send()


def shards(n, features, probes, bases, transfers, couplings, near_list, near_count):
    rows, feats = features.shape
    width = probes.shape[1]
    half = width // 2
    ranks = bases.shape[1]
    levels = transfers.shape[1]
    sends = CHUNKS + 2 * len(BLOCKS) + 17
    hbm = pl.BlockSpec(memory_space=pltpu.HBM)

    def vmem(*shape, dtype=F32):
        return pltpu.VMEM(shape, dtype)

    return pl.pallas_call(
        functools.partial(kernel, n),
        out_shape=jax.ShapeDtypeStruct((rows, width), F32),
        in_specs=[hbm] * 7,
        out_specs=pl.BlockSpec(memory_space=pltpu.VMEM),
        scratch_shapes=[
            vmem(rows, feats, dtype=BF16), vmem(rows, feats, dtype=BF16),
            vmem(rows, feats, dtype=BF16), vmem(rows, feats, dtype=BF16),
            vmem(rows, width), vmem(rows, width),
            vmem(rows, 2 * width, dtype=BF16), vmem(rows, width, dtype=BF16),
            vmem(rows, width, dtype=BF16), vmem(rows, width, dtype=BF16),
            vmem(rows, ranks), vmem(levels, ranks, ranks), vmem(levels + 1, ranks, ranks),
            vmem(width, ranks), vmem(width, ranks), vmem(width, ranks), vmem(half, ranks),
            vmem(half, ranks, dtype=BF16), vmem(half, ranks, dtype=BF16),
            vmem(half, ranks, dtype=BF16), vmem(2, half, ranks, dtype=BF16),
            vmem(half, ranks, dtype=BF16), vmem(3, half, ranks, dtype=BF16),
            vmem(5, half, ranks, dtype=BF16), vmem(half, ranks), vmem(half, ranks),
            vmem(rows, width, dtype=BF16), vmem(rows, width, dtype=BF16),
            vmem(rows, width),
            pltpu.SMEM((1, 4), jnp.int32), pltpu.SMEM((1,), jnp.int32),
            pltpu.SemaphoreType.DMA((7,)),
            pltpu.SemaphoreType.DMA((sends,)),
            pltpu.SemaphoreType.DMA((sends,)),
        ],
        compiler_params=pltpu.CompilerParams(
            collective_id=0, has_side_effects=True, vmem_limit_bytes=56 * 1024 * 1024),
    )(features, probes, bases, transfers[0], couplings[0], near_list, near_count)


def solution(mesh):
    in_specs = (
        P("leaf", None),
        P("leaf", None),
        P("leaf", None),
        P("leaf", None, None, None),
        P("leaf", None, None, None),
        P("leaf", None),
        P("leaf"),
    )
    return jax.shard_map(
        functools.partial(shards, mesh.shape["leaf"]),
        mesh=mesh, in_specs=in_specs, out_specs=P("leaf", None), check_vma=False)
```

time: 45 us -> 43.3 us (0.962); the launches traced: 44.4 us -> 43.2 us
  Pallas kernels: 42.1 us -> 40.8 us
    pallas_call x1, Pallas kernels: 42.1 us -> 40.8 us  [shards(): pl.pallas_call(functools.partial(kernel, n), out_shape=jax.ShapeDtypeStru...]
where the time goes in v3:
time: 43.3 us; the launch traced here: 43.2 us
  Pallas kernels  40.8 us (94%)
  local copies, waits for them, and re-layouts  1.67 us (4%)
  between operations  0.66 us (2%)
    pallas_call x1, Pallas kernels, shards(): pl.pallas_call(functools.partial(kernel, n), out_shape=jax.ShapeDtypeStru...  40.8 us
    unnamed x1, local copies, waits for them, and re-layouts  1.67 us

profile of v3, /device:TPU:6, one launch (start us, length us, event | category | flops | bytes accessed | tf_op | source)
XLA Modules:
  0.0 43.2 jit_solution(6838318096479641241)
XLA Ops:
  0.7 40.8 %shard_map.73 = f32[512,128]{1,0:T(8,128)} custom-call(bf16[512,1024]{1,0:T(8,128)(2,1)} %feat.1, f32[512,128]{1,0:T(8,128)} %prob.1, f32[512,256]{1,0:T(8,128)} %base.1, f32[4,256,256]{2,1,0:T(8,128)} %bitcast.3, f32[5,256,256]{2,1,0:T(8,128)} %bitcast.2, s32[1,4]{1,0:T(1,128)} %nlist_hbm.1, s32[1]{0:T(128)S(6)} %copy.9.ncount_hbm), custom_call_target="tpu_custom_call" | custom-call | tf_op jit(solution)/shard_map/pallas_call | solution.py:326
  41.5 1.7 %copy.10 = f32[512,128]{1,0:T(8,128)} copy(f32[512,128]{1,0:T(8,128)} %shard_map.73) | data formatting | bytes 524288

commit v4 on v3

--- a/solution.py
+++ b/solution.py
@@ -12,6 +12,7 @@
 CHUNKS = 16
 BLOCKS = ((0, 256), (256, 128), (384, 128))
 BURSTS = (5, 6, 7)
+FIRST_BURSTS = (18, 0, 0)
 
 NN = (((1,), (0,)), ((), ()))
 NT = (((1,), (1,)), ((), ()))
@@ -43,8 +44,8 @@
         else:
             pl.when(when)(act)
 
-    def start(self):
-        self.run(self.copy.start, self.sends)
+    def start(self, when=None):
+        self.run(self.copy.start, self.sends if when is None else jnp.logical_and(self.sends, when))
         return self
 
     def wait_send(self):
@@ -79,6 +80,8 @@
     level4, level4_far = me + flip(4), me + flip(2) + flip(3) + flip(4)
     early = lax.rem(me // 2, 8) < 4
     late = jnp.logical_not(early)
+    hurried = lax.rem(me, 16) == 0
+    row_end = lax.rem(me // 2, 8) == 7
 
     barrier = pltpu.get_barrier_semaphore()
 
@@ -169,11 +172,18 @@
     x_moves = [ahead(x_b.at[part(k, 2)], x_p.at[part(k, 2)]) for k in range(2)]
     waiting = phi_moves[:6] + x_moves + phi_moves[6:]
 
-    def burst(times):
-        for _ in range(times):
-            waiting.pop(0).start()
-
-    burst(BURSTS[0])
+    def burst(stage):
+        for k, m in enumerate(waiting):
+            plain = sum(BURSTS[:stage]) <= k < sum(BURSTS[:stage + 1])
+            sooner = sum(FIRST_BURSTS[:stage]) <= k < sum(FIRST_BURSTS[:stage + 1])
+            if plain and sooner:
+                m.start()
+            elif plain:
+                m.start(jnp.logical_not(hurried))
+            elif sooner:
+                m.start(hurried)
+
+    burst(0)
     o_moves = [send(feat.at[part(k, 2)], phi_o.at[part(k, 2)], other) for k in range(2)]
     xo_move = send(prob, x_o, other)
 
@@ -212,30 +222,32 @@
         xoh, xol = split(x_o[part(k, 2), :])
         acc[...] += m_o * apply_wide(th, tl, jnp.concatenate([xoh, xol], axis=1))
 
-    fwd, back = [], []
+    spans = [pl.ds(start, length) for start, length in BLOCKS]
+    xg_move = move(x_p, x_g, other)
+    fwd = [move(phi_p.at[at], phi_g.at[at], other) for at in spans]
+    back = [move(bk.at[at], bk_r.at[at], source, has_source, has_target) for at in spans]
 
     def far_pair(k):
         start, length = BLOCKS[k]
-        at = pl.ds(start, length)
+        at = spans[k]
         if k == 0:
             for m in x_moves:
                 m.wait_recv()
-            fwd.append(send(x_p, x_g, other))
+            xg_move.start()
         for m in phi_moves[start * CHUNKS // rows:(start + length) * CHUNKS // rows]:
             m.wait_recv()
-        fwd.append(send(phi_p.at[at], phi_g.at[at], other))
+        fwd[k].start()
         th, tl = tile_of(phi_p[at, :], phi_q[...])
         bk[at, :] = apply_wide(th, tl, x_cat[...]).astype(BF16)
-        back.append(send(bk.at[at], bk_r.at[at], source, has_source, has_target))
+        back[k].start()
         xs = x_p[at, :]
         acc[...] += m_p * (dot(th, xs, TN) + dot(tl, xs, TN))
 
     def near_pair(k):
-        start, length = BLOCKS[k]
-        at = pl.ds(start, length)
+        at = spans[k]
         if k == 0:
-            fwd[0].wait_recv()
-        fwd[k + 1].wait_recv()
+            xg_move.wait_recv()
+        fwd[k].wait_recv()
         th, tl = tile_of(phi_q[...], phi_g[at, :])
         xs = x_g[at, :]
         acc[...] += m_g * (dot(th, xs) + dot(tl, xs))
@@ -253,7 +265,7 @@
     v3_moves = [send(v3, v3_r.at[1], cross_next), send(v3, v3_r.at[0], cross)]
     ss[0] = s1.astype(BF16)
     s1_move = send(ss.at[0], ss_r.at[0], next_chip)
-    burst(BURSTS[1])
+    burst(1)
     pl.when(late)(ld_phi.wait)
     beside(0)
     beside(1)
@@ -274,7 +286,7 @@
     t4_moves = [send(t4, ss_r.at[4], level4_far), send(t4, ss_r.at[3], level4)]
     ss[2] = s3.astype(BF16)
     s3_move = send(ss.at[2], ss_r.at[2], level3)
-    burst(BURSTS[2])
+    burst(2)
 
     def couple(level, m):
         m.wait_recv()
@@ -287,6 +299,7 @@
     near_pair(0)
     coupled2 = couple(2, s2_move)
     far_pair(1)
+    pl.when(row_end)(lambda: far_pair(2))
     for m in t4_moves:
         m.wait_recv()
     e = g * dot3(ss_r[3].astype(F32) + ss_r[4].astype(F32), km[4], NT)
@@ -295,7 +308,7 @@
     e1[...] = coupled1 + factor(2) * dot3(e, tm[1], NT)
     e1_move = send(e1, e1_r, other)
     near_pair(1)
-    far_pair(2)
+    pl.when(jnp.logical_not(row_end))(lambda: far_pair(2))
     e1_move.wait_recv()
     mine, theirs = e1[...], e1_r[...]
     first = jnp.where(core == 0, mine, theirs)
@@ -307,7 +320,7 @@
     for m in back:
         m.wait_recv()
     out[...] = acc[...] + m_b * bk_r[...].astype(F32)
-    for m in phi_moves + x_moves + sent:
+    for m in phi_moves + x_moves + fwd + back + [xg_move] + sent:
         m.wait_send()
 
 

time: 43.3 us -> 43.1 us (level)
  no operation moved by 1% of the time
where the time goes in v4:
time: 43.1 us; the launch traced here: 42.9 us
  Pallas kernels  40.6 us (94%)
  local copies, waits for them, and re-layouts  1.67 us (4%)
  between operations  0.66 us (2%)
    pallas_call x1, Pallas kernels, shards(): pl.pallas_call(functools.partial(kernel, n), out_shape=jax.ShapeDtypeStru...  40.6 us
    unnamed x1, local copies, waits for them, and re-layouts  1.67 us

profile of v4, /device:TPU:6, one launch (start us, length us, event | category | flops | bytes accessed | tf_op | source)
XLA Modules:
  0.0 42.9 jit_solution(9134677603575911274)
XLA Ops:
  0.7 40.6 %shard_map.73 = f32[512,128]{1,0:T(8,128)} custom-call(bf16[512,1024]{1,0:T(8,128)(2,1)} %feat.1, f32[512,128]{1,0:T(8,128)} %prob.1, f32[512,256]{1,0:T(8,128)} %base.1, f32[4,256,256]{2,1,0:T(8,128)} %bitcast.3, f32[5,256,256]{2,1,0:T(8,128)} %bitcast.2, s32[1,4]{1,0:T(1,128)} %nlist_hbm.1, s32[1]{0:T(128)S(6)} %copy.9.ncount_hbm), custom_call_target="tpu_custom_call" | custom-call | tf_op jit(solution)/shard_map/pallas_call | solution.py:339
  41.3 1.7 %copy.10 = f32[512,128]{1,0:T(8,128)} copy(f32[512,128]{1,0:T(8,128)} %shard_map.73) | data formatting | bytes 524288

commit v5 on v4

--- a/solution.py
+++ b/solution.py
@@ -12,7 +12,6 @@
 CHUNKS = 16
 BLOCKS = ((0, 256), (256, 128), (384, 128))
 BURSTS = (5, 6, 7)
-FIRST_BURSTS = (18, 0, 0)
 
 NN = (((1,), (0,)), ((), ()))
 NT = (((1,), (1,)), ((), ()))
@@ -57,7 +56,7 @@
 
 def kernel(n, feat, prob, base, tran, coup, nlist_hbm, ncount_hbm, out,
            phi_q, phi_p, phi_g, phi_o, x_q, x_o, x_cat, x_b, x_p, x_g, u, tm, km,
-           s0, s0_r, t1, t1_r, t2, t2_r, v3, v3_r, t4, ss, ss_r, e1, e1_r, bk, bk_r, acc,
+           s0, s0_r, t1, t1_r, t2, t2_r, v3, v3_r, t4, ss, ss_r, e1, e1_r, bk, bk_r, acc, kept_h, kept_l,
            nlist, ncount, ld_sem, snd, rcv):
     me = lax.axis_index("leaf")
     core = lax.rem(me, 2)
@@ -174,13 +173,13 @@
 
     def burst(stage):
         for k, m in enumerate(waiting):
-            plain = sum(BURSTS[:stage]) <= k < sum(BURSTS[:stage + 1])
-            sooner = sum(FIRST_BURSTS[:stage]) <= k < sum(FIRST_BURSTS[:stage + 1])
-            if plain and sooner:
-                m.start()
-            elif plain:
-                m.start(jnp.logical_not(hurried))
-            elif sooner:
+            if sum(BURSTS[:stage]) <= k < sum(BURSTS[:stage + 1]):
+                if stage == 0:
+                    m.start()
+                else:
+                    m.start(jnp.logical_not(hurried))
+        if stage == 0:
+            for m in [m for m in waiting[BURSTS[0]:] if m not in x_moves] + x_moves:
                 m.start(hurried)
 
     burst(0)
@@ -227,21 +226,37 @@
     fwd = [move(phi_p.at[at], phi_g.at[at], other) for at in spans]
     back = [move(bk.at[at], bk_r.at[at], source, has_source, has_target) for at in spans]
 
+    def take_probes():
+        for m in x_moves:
+            m.wait_recv()
+        xg_move.start()
+
+    def kept_tiles():
+        take_probes()
+        xs = x_p[...]
+        acc[...] += m_p * (dot(kept_h[...], xs, TN) + dot(kept_l[...], xs, TN))
+
     def far_pair(k):
         start, length = BLOCKS[k]
         at = spans[k]
         if k == 0:
-            for m in x_moves:
-                m.wait_recv()
-            xg_move.start()
+            pl.when(jnp.logical_not(row_end))(take_probes)
         for m in phi_moves[start * CHUNKS // rows:(start + length) * CHUNKS // rows]:
             m.wait_recv()
         fwd[k].start()
         th, tl = tile_of(phi_p[at, :], phi_q[...])
         bk[at, :] = apply_wide(th, tl, x_cat[...]).astype(BF16)
         back[k].start()
-        xs = x_p[at, :]
-        acc[...] += m_p * (dot(th, xs, TN) + dot(tl, xs, TN))
+
+        @pl.when(row_end)
+        def _():
+            kept_h[at, :] = th
+            kept_l[at, :] = tl
+
+        @pl.when(jnp.logical_not(row_end))
+        def _():
+            xs = x_p[at, :]
+            acc[...] += m_p * (dot(th, xs, TN) + dot(tl, xs, TN))
 
     def near_pair(k):
         at = spans[k]
@@ -296,10 +311,16 @@
 
     coupled1 = couple(1, s1_move)
     far_pair(0)
-    near_pair(0)
+    pl.when(jnp.logical_not(row_end))(lambda: near_pair(0))
     coupled2 = couple(2, s2_move)
     far_pair(1)
-    pl.when(row_end)(lambda: far_pair(2))
+
+    @pl.when(row_end)
+    def _():
+        far_pair(2)
+        kept_tiles()
+        near_pair(0)
+
     for m in t4_moves:
         m.wait_recv()
     e = g * dot3(ss_r[3].astype(F32) + ss_r[4].astype(F32), km[4], NT)
@@ -354,7 +375,7 @@
             vmem(half, ranks, dtype=BF16), vmem(3, half, ranks, dtype=BF16),
             vmem(5, half, ranks, dtype=BF16), vmem(half, ranks), vmem(half, ranks),
             vmem(rows, width, dtype=BF16), vmem(rows, width, dtype=BF16),
-            vmem(rows, width),
+            vmem(rows, width), vmem(rows, rows, dtype=BF16), vmem(rows, rows, dtype=BF16),
             pltpu.SMEM((1, 4), jnp.int32), pltpu.SMEM((1,), jnp.int32),
             pltpu.SemaphoreType.DMA((7,)),
             pltpu.SemaphoreType.DMA((sends,)),

time: 43.1 us -> 41.7 us (0.968)
  Pallas kernels: 40.6 us -> 39.2 us
    pallas_call x1, Pallas kernels: 40.6 us -> 39.2 us  [shards(): pl.pallas_call(functools.partial(kernel, n), out_shape=jax.ShapeDtypeStru...]
where the time goes in v5:
time: 41.7 us; the launch traced here: 41.5 us
  Pallas kernels  39.2 us (94%)
  local copies, waits for them, and re-layouts  1.67 us (4%)
  between operations  0.66 us (2%)
    pallas_call x1, Pallas kernels, shards(): pl.pallas_call(functools.partial(kernel, n), out_shape=jax.ShapeDtypeStru...  39.2 us
    unnamed x1, local copies, waits for them, and re-layouts  1.67 us

profile of v5, /device:TPU:6, one launch (start us, length us, event | category | flops | bytes accessed | tf_op | source)
XLA Modules:
  0.0 41.5 jit_solution(18099960808255205084)
XLA Ops:
  0.7 39.2 %shard_map.73 = f32[512,128]{1,0:T(8,128)} custom-call(bf16[512,1024]{1,0:T(8,128)(2,1)} %feat.1, f32[512,128]{1,0:T(8,128)} %prob.1, f32[512,256]{1,0:T(8,128)} %base.1, f32[4,256,256]{2,1,0:T(8,128)} %bitcast.3, f32[5,256,256]{2,1,0:T(8,128)} %bitcast.2, s32[1,4]{1,0:T(1,128)} %nlist_hbm.1, s32[1]{0:T(128)S(6)} %copy.9.ncount_hbm), custom_call_target="tpu_custom_call" | custom-call | tf_op jit(solution)/shard_map/pallas_call | solution.py:360
  39.8 1.7 %copy.10 = f32[512,128]{1,0:T(8,128)} copy(f32[512,128]{1,0:T(8,128)} %shard_map.73) | data formatting | bytes 524288
